TPU v7x, 128 devices: a whole 4x4x4 slice. The times are simulated.
128 devices in a mesh: row: 16 (over x, y), col: 8 (over z, core).
Axes of the slice: x: 4, y: 4, z: 4, core: 2. Of those that a mesh axis runs over, the one named last changes fastest.
Arguments:
- residual: bfloat16 [1024, 16, 5120], P('row', None, 'col'), may hold values from -6 to 6
- positions: int32 [1024], P('row'), may hold values from 0 to 15
- norm_gain: float32 [5120], P('col'), may hold values from 0.1 to 1.9
- w_gate: bfloat16 [5120, 16384], P('col', 'row'), may hold values from -0.078125 to 0.078125
- w_up: bfloat16 [5120, 16384], P('col', 'row'), may hold values from -0.078125 to 0.078125
- covariance: float32 [16384, 16384], P('row', 'col'), may hold values from -1 to 4, as said below
Outputs:
- factor: float32 [16384, 16384], P('row', 'col')
Inputs may be any that keep to these rules, and one draw needn't show every extreme that they name: `covariance`: symmetric positive definite in the natural order of hidden units.
All inputs are finite; a program needn't handle non-finite values.
Results may differ from a plain program's by a relative error of at most 0.0041.
Values may be sent and summed in bfloat16 or wider, within the bound.
A program may use at most 128 MiB of HBM per device.

v0:
```python
import functools
import jax
import jax.numpy as jnp
from jax import lax
from jax.sharding import Mesh
from jax.sharding import PartitionSpec as P

TILE = 64
PANEL = 256
NPANEL = 2
ROW = ("row_0", "row_1")
EPSILON = 1e-06
HIGHEST_PRECISION = lax.Precision.HIGHEST


def by_axis(array, axes):
    return functools.reduce(lax.psum, axes, array)


def copy_for_each(array, axis):
    copies = jnp.broadcast_to(array, (lax.axis_size(axis), *array.shape))
    return lax.all_to_all(copies, axis, split_axis=0, concat_axis=0, tiled=True)


def of_everyone(array, axis):
    everything = copy_for_each(array, axis)
    return jnp.sum(everything, axis=0)


def joined_along(pieces, dim):
    lengths = list(pieces.shape[1:])
    lengths[dim] *= pieces.shape[0]
    return jnp.moveaxis(pieces, 0, dim).reshape(lengths)


def gathered_copies(array, axis, dim):
    return joined_along(copy_for_each(array, axis), dim)


def shortened(array):

    def short(part):
        return part.astype(jnp.bfloat16) if part.dtype == jnp.float32 else part

    return jax.tree.map(short, array)


def broadcast(value, axis, source):
    kept = jnp.where(lax.axis_index(axis) == source, value, 0).astype(value.dtype)
    return lax.psum(kept, axis)


def trailing(left_factor, right_factor):
    return lax.dot_general(
        left_factor,
        right_factor,
        (((1,), (1,)), ((), ())),
        precision=HIGHEST_PRECISION,
        preferred_element_type=jnp.float32,
    )


def unit_scale(raw_keys, wide_hidden):
    squares = by_axis(jnp.sum(raw_keys * raw_keys, axis=1), ROW)
    return (raw_keys * lax.rsqrt(squares / wide_hidden + EPSILON)[:, None]).astype(jnp.bfloat16)


def on_device(residual, positions, norm_gain, w_gate, w_up, covariance):
    row_devices = lax.axis_size(ROW)
    col_devices = lax.axis_size("col")
    row_rank = lax.axis_index(ROW)
    col_rank = lax.axis_index("col")
    local_prompts = residual.shape[0]
    token_count = residual.shape[1]
    local_feat = residual.shape[2]
    model_width = local_feat * col_devices
    hidden_local = w_gate.shape[1]
    wide_hidden = hidden_local * row_devices
    row_count = covariance.shape[0]
    col_count = covariance.shape[1]
    tiles_here = hidden_local // TILE
    panel_tiles = PANEL // TILE
    token_iota = lax.broadcasted_iota(jnp.int32, (local_prompts, token_count), 1)
    token_mask = (token_iota == positions[:, None])[:, :, None]
    picked = jnp.where(token_mask, residual, jnp.zeros_like(residual))
    subject = jnp.sum(picked.astype(jnp.float32), axis=1)
    part_squares = jnp.sum(subject * subject, axis=1)
    total_squares = of_everyone(part_squares, "col")
    inverse_rms = lax.rsqrt(total_squares / model_width + EPSILON)
    normed = (subject * inverse_rms[:, None] * norm_gain[None, :]).astype(jnp.bfloat16)
    normed_all = gathered_copies(normed, ROW, 0)
    prompts = normed_all.shape[0]
    gate_block = jnp.dot(normed_all, w_gate, preferred_element_type=jnp.float32)
    up_block = jnp.dot(normed_all, w_up, preferred_element_type=jnp.float32)
    shared = lax.psum_scatter(
        jnp.concatenate([gate_block, up_block], axis=1), "col", scatter_dimension=0, tiled=True
    )
    unit_share = unit_scale(
        jax.nn.silu(shared[:, :hidden_local]) * shared[:, hidden_local:], wide_hidden
    )
    unit_keys = gathered_copies(unit_share, "col", 0)
    grouped = (
        unit_keys.reshape(prompts, tiles_here // row_devices, row_devices, TILE)
        .transpose(0, 2, 1, 3)
        .reshape(prompts, hidden_local)
    )
    row_keys = lax.all_to_all(grouped, ROW, split_axis=1, concat_axis=1, tiled=True)
    col_split = unit_keys.reshape(prompts, tiles_here // col_devices, col_devices, TILE)
    col_pick = lax.dynamic_index_in_dim(col_split, col_rank, axis=2, keepdims=False).reshape(
        prompts, tiles_here // col_devices * TILE
    )
    col_keys = lax.all_gather(col_pick, ROW, axis=1, tiled=True)
    keys_outer = lax.dot_general(
        row_keys, col_keys, (((0,), (0,)), ((), ())), preferred_element_type=jnp.float32
    )
    updated = covariance + keys_outer * (1.0 / prompts)
    row_pos = lax.broadcasted_iota(jnp.int32, (row_count,), 0)
    row_global = (row_pos // TILE * row_devices + row_rank) * TILE + row_pos % TILE
    col_pos = lax.broadcasted_iota(jnp.int32, (col_count,), 0)
    col_global = (col_pos // TILE * col_devices + col_rank) * TILE + col_pos % TILE
    row_groups = row_devices // col_devices
    panel_iota = lax.broadcasted_iota(jnp.int32, (1, PANEL), 1)

    def col_bounds(number):
        first_tile = number * panel_tiles
        col_start = first_tile // col_devices
        col_end = (first_tile + panel_tiles - 1) // col_devices + 1
        return (col_start * TILE, col_end * TILE)

    for number in range(NPANEL):
        begin_col, end_col = col_bounds(number)
        factor_first_tile = number * panel_tiles
        factor_col_start = factor_first_tile // col_devices
        col_tiles = (factor_first_tile + panel_tiles - 1) // col_devices + 1 - factor_col_start
        gathered = gathered_copies(updated[:, begin_col:end_col], "col", 1)
        gathered = (
            gathered.reshape(row_count, col_devices, col_tiles, TILE)
            .transpose(0, 2, 1, 3)
            .reshape(row_count, col_tiles * col_devices * TILE)
        )
        col_offset = (factor_first_tile - factor_col_start * col_devices) * TILE
        panel_rows = gathered[:, col_offset : col_offset + PANEL]
        row_start = factor_first_tile // row_devices
        row_tiles = (factor_first_tile + panel_tiles - 1) // row_devices + 1 - row_start
        diag_rows = gathered_copies(
            panel_rows[row_start * TILE : (row_start + row_tiles) * TILE].astype(jnp.bfloat16),
            ROW,
            0,
        ).astype(jnp.float32)
        diag_rows = (
            diag_rows.reshape(row_devices, row_tiles, TILE, PANEL)
            .transpose(1, 0, 2, 3)
            .reshape(row_tiles * row_devices * TILE, PANEL)
        )
        row_offset = (factor_first_tile - row_start * row_devices) * TILE
        lower_factor = jnp.linalg.cholesky(diag_rows[row_offset : row_offset + PANEL])
        solved = jax.scipy.linalg.solve_triangular(lower_factor, panel_rows.T, lower=True).T
        factor_shifted = row_global - number * PANEL
        selector = (factor_shifted[:, None] == panel_iota).astype(jnp.float32)
        from_lower = jnp.dot(
            selector, lower_factor, precision=HIGHEST_PRECISION, preferred_element_type=jnp.float32
        )
        factor_panel_factor = jnp.where((factor_shifted >= PANEL)[:, None], solved, from_lower)
        received = []
        for member in range(row_groups):
            received.append(
                broadcast(
                    shortened(factor_panel_factor), ROW, col_rank + member * col_devices
                ).astype(factor_panel_factor.dtype)
            )
        column_factor = (
            jnp.stack(received, 0)
            .reshape(row_groups, row_count // TILE, TILE, PANEL)
            .transpose(1, 0, 2, 3)
            .reshape(col_count, PANEL)
        )
        panel_factor, column_factor = (factor_panel_factor, column_factor)
        updated = updated - trailing(panel_factor, column_factor)
        place_begin_col, place_end_col = col_bounds(number)
        shifted = col_global[place_begin_col:place_end_col] - number * PANEL
        within = (shifted >= 0) & (shifted < PANEL)
        column_select = (panel_iota[0][:, None] == shifted[None, :]).astype(jnp.float32)
        values = jnp.dot(
            panel_factor,
            column_select,
            precision=HIGHEST_PRECISION,
            preferred_element_type=jnp.float32,
        )
        replaced = jnp.where(within[None, :], values, updated[:, place_begin_col:place_end_col])
        updated = updated.at[:, place_begin_col:place_end_col].set(replaced)
    lower_part = row_global[:, None] >= col_global[None, :]
    return jnp.where(lower_part, updated, 0.0)


def solution(mesh):
    torus = Mesh(mesh.devices.reshape(4, 4, mesh.shape["col"]), ("row_0", "row_1", "col"))
    placed = (P(ROW, None, "col"), P(ROW), P("col"), P("col", ROW), P("col", ROW), P(ROW, "col"))
    return jax.shard_map(
        on_device, mesh=torus, in_specs=placed, out_specs=P(ROW, "col"), check_vma=False
    )
```

profile of v0, /device:TPU:0, one launch (start us, length us, event | category | flops | bytes accessed | tf_op | source)
XLA Modules:
  0.0 690.5 jit_solution(8219200208824315445)
XLA Ops:
  10.1 5.4 all-to-all-start
  15.6 5.1 all-to-all-done
  21.7 26.6 %all_to_all.48 = bf16[16,64,640]{2,1,0:T(8,128)(2,1)S(1)} all-to-all(bf16[16,64,640]{2,1,0:T(8,128)(2,1)S(1)} %broadcast_in_dim.88), channel_id=1, replica_groups=mesh['row_0'=4,'row_1'=4,'col'=8] {'row_0','row_1'}, dimensions={0} | all-to-all | bytes 2621440 | tf_op jit(solution)/shard_map/all_to_all | solution.py:22
  56.2 49.1 %reduce-scatter.2.cloned.1.call-done = f32[128,2048]{0,1:T(8,128)} async-done(((f32[1024,2048]{0,1:T(8,128)}), f32[128,2048]{0,1:T(8,128)}) %reduce-scatter.2.cloned.1.call-update) | async-done | bytes 1048592 | tf_op jit(solution)/shard_map/reduce_scatter | solution.py:95
  106.7 10.4 %psum.42 = f32[128]{0:T(128)S(1)} all-reduce(f32[128]{0:T(128)S(1)} %get-tuple-element.67), channel_id=1, replica_groups=mesh['row_0'=4,'row_1'=4,'col'=8] {'row_0'}, use_global_device_ids=true, to_apply=%region_5.6 | all-reduce | flops 128 | bytes 1024 | tf_op jit(solution)/shard_map/psum | solution.py:17
  117.1 10.5 %psum.43 = f32[128]{0:T(128)S(1)} all-reduce(f32[128]{0:T(128)S(1)} %psum.42), channel_id=1, replica_groups=mesh['row_0'=4,'row_1'=4,'col'=8] {'row_1'}, use_global_device_ids=true, to_apply=%region_6.7 | all-reduce | flops 128 | bytes 1024 | tf_op jit(solution)/shard_map/psum | solution.py:17
  129.2 4.3 all-to-all-start.2
  133.6 27.1 %all-to-all-done.2 = bf16[8,128,1024]{1,2,0:T(8,128)(2,1)} async-done(((bf16[8,128,1024]{1,2,0:T(8,128)(2,1)}), bf16[8,128,1024]{1,2,0:T(8,128)(2,1)}, u32[]{:S(2)}, u32[]{:S(2)}) %all-to-all-start.2) | async-done | bytes 2097184 | tf_op jit(solution)/shard_map/all_to_all | solution.py:22
  170.0 35.8 %all_to_all.49 = bf16[1024,16,64]{0,2,1:T(8,128)(2,1)S(1)} all-to-all(bf16[1024,16,64]{0,2,1:T(8,128)(2,1)} %all_to_all.33), channel_id=1, replica_groups=mesh['row_0'=4,'row_1'=4,'col'=8] {'row_0','row_1'}, dimensions={1} | all-to-all | bytes 4194304 | tf_op jit(solution)/shard_map/all_to_all | solution.py:107
  205.8 24.1 %all-gather.2.cloned.1.call-done = bf16[1024,2048]{0,1:T(8,128)(2,1)} async-done(((bf16[1024,128]{0,1:T(8,128)(2,1)}), bf16[1024,2048]{0,1:T(8,128)(2,1)}) %all-gather.2.cloned.1.call-update) | async-done | bytes 4194320 | tf_op jit(solution)/shard_map/all_gather | solution.py:112
  229.9 8.2 %multiply_add_fusion = f32[1024,2048]{1,0:T(8,128)S(1)} fusion(f32[1024,2048]{1,0:T(8,128)} %param.18, bf16[1024,1024]{0,1:T(8,128)(2,1)S(1)} %bitcast.126, bf16[1024,2048]{0,1:T(8,128)(2,1)} %all-gather.2.cloned.1.call-done), kind=kOutput, calls=%fused_computation.5 | convolution fusion | flops 4299161600 | bytes 23068672 | tf_op jit(solution)/shard_map/dot_general | solution.py:113
  243.4 4.6 all-to-all-start.4
  248.1 27.1 %all-to-all-done.4 = f32[8,1024,64]{1,2,0:T(8,128)S(1)} async-done(((f32[8,1024,64]{1,2,0:T(8,128)}), f32[8,1024,64]{1,2,0:T(8,128)S(1)}, u32[]{:S(2)}, u32[]{:S(2)}) %all-to-all-start.4) | async-done | bytes 2097184 | tf_op jit(solution)/shard_map/all_to_all | solution.py:22
  276.2 5.3 all-to-all-start.5
  281.6 11.2 %all-to-all-done.5 = bf16[16,64,256]{2,1,0:T(8,128)(2,1)} async-done(((bf16[16,64,256]{2,1,0:T(8,128)(2,1)}), bf16[16,64,256]{2,1,0:T(8,128)(2,1)}, u32[]{:S(2)}, u32[]{:S(2)}) %all-to-all-start.5) | async-done | bytes 524320 | tf_op jit(solution)/shard_map/all_to_all | solution.py:22
  294.0 11.7 %cholesky.130 = f32[128,128]{1,0:T(8,128)S(1)} custom-call(f32[128,128]{1,0:T(8,128)S(1)} %cholesky.194), custom_call_target="Cholesky" | custom-call | tf_op jit(solution)/shard_map/jit(cholesky)/cholesky | solution.py:156
  305.7 9.8 %custom-call.13 = f32[1,128,128]{1,2,0:T(8,128)S(1)} custom-call(f32[1,128,128]{2,1,0:T(8,128)S(1)} %get-tuple-element.84), custom_call_target="InvertDiagBlocksLowerTriangular" | custom-call | tf_op jit(solution)/shard_map/jit(cholesky)/cholesky | solution.py:156
  316.0 11.7 %cholesky.147 = f32[128,128]{1,0:T(8,128)S(1)} custom-call(f32[128,128]{1,0:T(8,128)S(1)} %convolution_subtract_fusion.5), custom_call_target="Cholesky" | custom-call | tf_op jit(solution)/shard_map/jit(cholesky)/cholesky | solution.py:156
  329.9 4.3 while.6
  334.2 19.7 %custom-call.14 = f32[2,128,128]{1,2,0:T(8,128)S(1)} custom-call(f32[2,128,128]{2,1,0:T(8,128)S(1)} %get-tuple-element.45), custom_call_target="InvertDiagBlocksLowerTriangular" | custom-call | tf_op jit(solution)/shard_map/jit(_solve_triangular)/triangular_solve | solution.py:157
  359.3 82.4 %all-reduce.8.cloned.1.call-done = (bf16[1,16,64,256]{3,2,1,0:T(8,128)(2,1)}, bf16[1,16,64,256]{3,2,1,0:T(8,128)(2,1)}) async-done(((bf16[1,16,64,256]{3,2,1,0:T(8,128)(2,1)}, bf16[1,16,64,256]{3,2,1,0:T(8,128)(2,1)}), (bf16[1,16,64,256]{3,2,1,0:T(8,128)(2,1)}, bf16[1,16,64,256]{3,2,1,0:T(8,128)(2,1)})) %all-reduce.8.cloned.1.call-update) | async-done | bytes 1048592 | tf_op jit(solution)/shard_map/psum | solution.py:50
  443.1 9.5 %convolution_subtract_fusion.1 = f32[1024,2048]{1,0:T(8,128)S(1)} fusion(f32[1024,2048]{1,0:T(8,128)} %copy-done.4, f32[1024,256]{0,1:T(8,128)S(1)} %get-tuple-element.91, bf16[2048,256]{1,0:T(8,128)(2,1)S(1)} %bitcast.124), kind=kOutput, calls=%fused_computation.8 | convolution fusion | flops 6444548096 | bytes 18874368 | tf_op jit(solution)/shard_map/dot_general | solution.py:54
  458.6 31.7 %all_to_all.50 = f32[8,1024,64]{1,2,0:T(8,128)S(1)} all-to-all(f32[8,1024,64]{1,2,0:T(8,128)S(1)} %broadcast_in_dim.96), channel_id=1, replica_groups=mesh['row_0'=4,'row_1'=4,'col'=8] {'col'}, dimensions={0} | all-to-all | bytes 4194304 | tf_op jit(solution)/shard_map/all_to_all | solution.py:22
  491.4 4.8 all-to-all-start.7
  496.7 10.6 %all-to-all-done.7 = bf16[16,64,256]{2,1,0:T(8,128)(2,1)} async-done(((bf16[16,64,256]{2,1,0:T(8,128)(2,1)}), bf16[16,64,256]{2,1,0:T(8,128)(2,1)}, u32[]{:S(2)}, u32[]{:S(2)}) %all-to-all-start.7) | async-done | bytes 524320 | tf_op jit(solution)/shard_map/all_to_all | solution.py:22
  508.5 11.7 %cholesky.164 = f32[128,128]{1,0:T(8,128)S(1)} custom-call(f32[128,128]{1,0:T(8,128)S(1)} %cholesky.197), custom_call_target="Cholesky" | custom-call | tf_op jit(solution)/shard_map/jit(cholesky)/cholesky | solution.py:156
  520.3 9.8 %custom-call.15 = f32[1,128,128]{1,2,0:T(8,128)S(1)} custom-call(f32[1,128,128]{2,1,0:T(8,128)S(1)} %get-tuple-element.80), custom_call_target="InvertDiagBlocksLowerTriangular" | custom-call | tf_op jit(solution)/shard_map/jit(cholesky)/cholesky | solution.py:156
  530.6 11.7 %cholesky.181 = f32[128,128]{1,0:T(8,128)S(1)} custom-call(f32[128,128]{1,0:T(8,128)S(1)} %convolution_subtract_fusion.4), custom_call_target="Cholesky" | custom-call | tf_op jit(solution)/shard_map/jit(cholesky)/cholesky | solution.py:156
  549.3 19.7 %custom-call.16 = f32[2,128,128]{1,2,0:T(8,128)S(1)} custom-call(f32[2,128,128]{2,1,0:T(8,128)S(1)} %get-tuple-element.46), custom_call_target="InvertDiagBlocksLowerTriangular" | custom-call | tf_op jit(solution)/shard_map/jit(_solve_triangular)/triangular_solve | solution.py:157
  577.2 79.6 %all-reduce.6.cloned.1.call-done = (bf16[1,16,64,256]{3,2,1,0:T(8,128)(2,1)}, bf16[1,16,64,256]{3,2,1,0:T(8,128)(2,1)}) async-done(((bf16[1,16,64,256]{3,2,1,0:T(8,128)(2,1)}, bf16[1,16,64,256]{3,2,1,0:T(8,128)(2,1)}), (bf16[1,16,64,256]{3,2,1,0:T(8,128)(2,1)}, bf16[1,16,64,256]{3,2,1,0:T(8,128)(2,1)})) %all-reduce.6.cloned.1.call-update) | async-done | bytes 1048592 | tf_op jit(solution)/shard_map/psum | solution.py:50
  658.2 9.5 %convolution_subtract_fusion = f32[1024,2048]{1,0:T(8,128)S(1)} fusion(f32[1024,2048]{1,0:T(8,128)} %scatter.6, f32[1024,256]{0,1:T(8,128)S(1)} %get-tuple-element.94, bf16[2048,256]{1,0:T(8,128)(2,1)S(1)} %bitcast.125), kind=kOutput, calls=%fused_computation.7 | convolution fusion | flops 6444548096 | bytes 18874368 | tf_op jit(solution)/shard_map/dot_general | solution.py:54
  676.2 7.6 %compare_select_fusion = f32[1024,2048]{1,0:T(8,128)} fusion(f32[1024,2048]{1,0:T(8,128)} %scatter.9, s32[2048]{0:T(1024)S(1)} %fusion.41, s32[1024]{0:T(1024)S(1)} %get-tuple-element.95), kind=kLoop, calls=%fused_computation.6 | loop fusion | flops 4194304 | bytes 16789504 | tf_op jit(solution)/shard_map/jit(_where)/select_n | solution.py:192
  (124 shorter events, 81.5 us)
Async XLA Ops:
  6.5 41.7 %copy-start = (bf16[640,1024]{1,0:T(8,128)(2,1)S(1)}, bf16[640,1024]{1,0:T(8,128)(2,1)}, u32[]{:S(2)}) copy-start(bf16[640,1024]{1,0:T(8,128)(2,1)} %param.17) | copy-start | bytes 3932164
  10.1 10.6 %all-to-all-start = ((f32[8,1,64]{2,1,0:T(1,128)}), f32[8,1,64]{2,1,0:T(1,128)S(1)}, u32[]{:S(2)}, u32[]{:S(2)}) async-start(f32[8,1,64]{2,1,0:T(1,128)} %broadcast_in_dim.87), calls=%async_computation | async-start | bytes 8192 | tf_op jit(solution)/shard_map/all_to_all | solution.py:22
  15.5 89.8 %reduce-scatter.2.cloned.1.call-start = ((), (), s32[]{:S(2)}) async-start(), calls=%async_computation.9 | async-start | bytes 9437184 | tf_op jit(solution)/shard_map/reduce_scatter | solution.py:95
  48.2 1.9 copy-start.7
  129.2 31.5 %all-to-all-start.2 = ((bf16[8,128,1024]{1,2,0:T(8,128)(2,1)}), bf16[8,128,1024]{1,2,0:T(8,128)(2,1)}, u32[]{:S(2)}, u32[]{:S(2)}) async-start(bf16[8,128,1024]{1,2,0:T(8,128)(2,1)} %broadcast_in_dim.89), calls=%async_computation.3 | async-start | bytes 4194304 | tf_op jit(solution)/shard_map/all_to_all | solution.py:22
  133.6 96.3 %all-gather.2.cloned.1.call-start = ((), (), s32[]{:S(2)}) async-start(), calls=%async_computation.10 | async-start | bytes 4456448 | tf_op jit(solution)/shard_map/all_gather | solution.py:112
  238.1 3.4 copy-start.4
  243.4 31.8 %all-to-all-start.4 = ((f32[8,1024,64]{1,2,0:T(8,128)}), f32[8,1024,64]{1,2,0:T(8,128)S(1)}, u32[]{:S(2)}, u32[]{:S(2)}) async-start(f32[8,1024,64]{1,2,0:T(8,128)} %broadcast_in_dim.91), calls=%async_computation.5 | async-start | bytes 4194304 | tf_op jit(solution)/shard_map/all_to_all | solution.py:22
  276.2 16.7 %all-to-all-start.5 = ((bf16[16,64,256]{2,1,0:T(8,128)(2,1)}), bf16[16,64,256]{2,1,0:T(8,128)(2,1)}, u32[]{:S(2)}, u32[]{:S(2)}) async-start(bf16[16,64,256]{2,1,0:T(8,128)(2,1)} %broadcast_in_dim.92), calls=%async_computation.6 | async-start | bytes 1048576 | tf_op jit(solution)/shard_map/all_to_all | solution.py:22
  281.5 160.2 %all-reduce.8.cloned.1.call-start = ((), (), s32[]{:S(2)}) async-start(), calls=%async_computation.12 | async-start | bytes 2097152 | tf_op jit(solution)/shard_map/psum | solution.py:50
  452.6 3.4 copy-start.2
  457.6 0.8 copy-start.5
  491.4 16.0 %all-to-all-start.7 = ((bf16[16,64,256]{2,1,0:T(8,128)(2,1)}), bf16[16,64,256]{2,1,0:T(8,128)(2,1)}, u32[]{:S(2)}, u32[]{:S(2)}) async-start(bf16[16,64,256]{2,1,0:T(8,128)(2,1)} %broadcast_in_dim.97), calls=%async_computation.8 | async-start | bytes 1048576 | tf_op jit(solution)/shard_map/all_to_all | solution.py:22
  496.2 160.7 %all-reduce.6.cloned.1.call-start = ((), (), s32[]{:S(2)}) async-start(), calls=%async_computation.11 | async-start | bytes 2097152 | tf_op jit(solution)/shard_map/psum | solution.py:50
  570.2 3.6 copy-start.6
  667.7 3.4 copy-start.3
  676.2 7.6 %copy-start.1 = (bf16[640,1024]{1,0:T(8,128)(2,1)S(1)}, bf16[640,1024]{1,0:T(8,128)(2,1)}, u32[]{:S(2)}) copy-start(bf16[640,1024]{1,0:T(8,128)(2,1)} %param.17) | copy-start | bytes 3932164
Sparse Core Ops, SparseCore 0:
  56.4 48.8 reduce-scatter.1
  167.8 62.0 all-gather.1
  358.8 82.9 all-reduce.7
  573.9 82.8 all-reduce.5
where the time goes:
time: 700 us; the launch traced here: 690 us
  waiting for transfers between devices  316 us (45%)
  other arithmetic  129 us (18%)
  blocking collectives  115 us (16%)
  local copies, waits for them, and re-layouts  48.1 us (7%)
  matrix products  40.5 us (6%)
  starting transfers between devices  25 us (4%)
  between operations  16.4 us (2%)
    psum x2, waiting for transfers between devices, broadcast(): return lax.psum(kept, axis)  162 us
    all_to_all x5, waiting for transfers between devices, copy_for_each(): return lax.all_to_all(copies, axis, split_axis=0, concat_axis=0, tiled=True)  81.3 us
    another operation x13, other arithmetic, on_device(): lower_factor = jnp.linalg.cholesky(diag_rows[row_offset:row_offset + PANEL])  68.7 us
    all_to_all x2, blocking collectives, copy_for_each(): return lax.all_to_all(copies, axis, split_axis=0, concat_axis=0, tiled=True)  58.3 us
    reduce_scatter x1, waiting for transfers between devices, on_device(): lax.psum_scatter(jnp.concatenate([gate_block, up_block], axis=1), 'col',...  49.1 us
    another operation x5, other arithmetic, on_device(): jax.scipy.linalg.solve_triangular(lower_factor, panel_rows.T, lower=True)  39.4 us
    all_to_all x1, blocking collectives, on_device(): lax.all_to_all(grouped, ROW, split_axis=1, concat_axis=1, tiled=True)  35.8 us
    all_to_all x5, starting transfers between devices, copy_for_each(): return lax.all_to_all(copies, axis, split_axis=0, concat_axis=0, tiled=True)  24.4 us
  transfers between devices with their start and end apart: 9, of which 9 were waited for; matrix products, arithmetic and copies ran while one was open for 1% of the time, Pallas kernels for 0%

commit v1 on v0

--- a/solution.py
+++ b/solution.py
@@ -109,7 +109,9 @@
     col_pick = lax.dynamic_index_in_dim(col_split, col_rank, axis=2, keepdims=False).reshape(
         prompts, tiles_here // col_devices * TILE
     )
-    col_keys = lax.all_gather(col_pick, ROW, axis=1, tiled=True)
+    col_keys = jnp.concatenate(
+        lax.all_to_all(jnp.stack([col_pick] * lax.axis_size(ROW)), ROW, 0, 0), axis=1
+    )
     keys_outer = lax.dot_general(
         row_keys, col_keys, (((0,), (0,)), ((), ())), preferred_element_type=jnp.float32
     )

time: 700 us -> 716 us (1.023)
  blocking collectives: 115 us -> 161 us
  waiting for transfers between devices: 316 us -> 292 us
    all_to_all x2 -> x3, blocking collectives: 58.3 us -> 88.2 us  [copy_for_each(): return lax.all_to_all(copies, axis, split_axis=0, concat_axis=0, tiled=True)]
    all_to_all x0 -> x1, waiting for transfers between devices: none -> 26.9 us  [on_device(): lax.all_to_all(grouped, ROW, split_axis=1, concat_axis=1, tiled=True)]
    all_to_all x5 -> x4, waiting for transfers between devices: 81.3 us -> 54.4 us  [copy_for_each(): return lax.all_to_all(copies, axis, split_axis=0, concat_axis=0, tiled=True)]
    all_gather x1 -> x0, waiting for transfers between devices: 24.1 us -> none  [on_device(): col_keys = lax.all_gather(col_pick, ROW, axis=1, tiled=True)]
    all_to_all x1, blocking collectives: 35.8 us -> 52.3 us  [on_device(): lax.all_to_all(jnp.stack([col_pick] * lax.axis_size(ROW)), ROW, 0, 0)]
    all_to_all x5 -> x4, starting transfers between devices: 24.4 us -> 18.4 us  [copy_for_each(): return lax.all_to_all(copies, axis, split_axis=0, concat_axis=0, tiled=True)]
  transfers between devices with their start and end apart: 9 -> 8, of which waited for: 9 -> 8; matrix products, arithmetic and copies ran while one was open for 1% -> 1% of each run, Pallas kernels for 0% -> 0%
where the time goes in v1:
time: 716 us; the launch traced here: 708 us
  waiting for transfers between devices  292 us (41%)
  blocking collectives  161 us (22%)
  other arithmetic  129 us (18%)
  local copies, waits for them, and re-layouts  45.1 us (6%)
  matrix products  40 us (6%)
  starting transfers between devices  23.3 us (3%)
  between operations  16.4 us (2%)
    psum x2, waiting for transfers between devices, broadcast(): return lax.psum(kept, axis)  162 us
    all_to_all x3, blocking collectives, copy_for_each(): return lax.all_to_all(copies, axis, split_axis=0, concat_axis=0, tiled=True)  88.2 us
    another operation x13, other arithmetic, on_device(): lower_factor = jnp.linalg.cholesky(diag_rows[row_offset:row_offset + PANEL])  68.7 us
    all_to_all x4, waiting for transfers between devices, copy_for_each(): return lax.all_to_all(copies, axis, split_axis=0, concat_axis=0, tiled=True)  54.4 us
    all_to_all x1, blocking collectives, on_device(): lax.all_to_all(jnp.stack([col_pick] * lax.axis_size(ROW)), ROW, 0, 0)  52.3 us
    reduce_scatter x1, waiting for transfers between devices, on_device(): lax.psum_scatter(jnp.concatenate([gate_block, up_block], axis=1), 'col',...  49.1 us
    another operation x5, other arithmetic, on_device(): jax.scipy.linalg.solve_triangular(lower_factor, panel_rows.T, lower=True)  39.4 us
    all_to_all x1, waiting for transfers between devices, on_device(): lax.all_to_all(grouped, ROW, split_axis=1, concat_axis=1, tiled=True)  26.9 us
  transfers between devices with their start and end apart: 8, of which 8 were waited for; matrix products, arithmetic and copies ran while one was open for 1% of the time, Pallas kernels for 0%

profile of v1, /device:TPU:0, one launch (start us, length us, event | category | flops | bytes accessed | tf_op | source)
XLA Modules:
  0.0 707.6 jit_solution(16466762456083549275)
XLA Ops:
  10.1 5.4 all-to-all-start
  15.6 5.1 all-to-all-done
  21.7 26.6 %all_to_all.53 = bf16[16,64,640]{2,1,0:T(8,128)(2,1)S(1)} all-to-all(bf16[16,64,640]{2,1,0:T(8,128)(2,1)S(1)} %broadcast_in_dim.88), channel_id=1, replica_groups=mesh['row_0'=4,'row_1'=4,'col'=8] {'row_0','row_1'}, dimensions={0} | all-to-all | bytes 2621440 | tf_op jit(solution)/shard_map/all_to_all | solution.py:22
  52.0 4.2 pad_maximum_fusion
  56.2 49.1 %reduce-scatter.2.cloned.1.call-done = f32[128,2048]{0,1:T(8,128)} async-done(((f32[1024,2048]{0,1:T(8,128)}), f32[128,2048]{0,1:T(8,128)}) %reduce-scatter.2.cloned.1.call-update) | async-done | bytes 1048592 | tf_op jit(solution)/shard_map/reduce_scatter | solution.py:95
  106.7 10.4 %psum.42 = f32[128]{0:T(128)S(1)} all-reduce(f32[128]{0:T(128)S(1)} %get-tuple-element.67), channel_id=1, replica_groups=mesh['row_0'=4,'row_1'=4,'col'=8] {'row_0'}, use_global_device_ids=true, to_apply=%region_5.6 | all-reduce | flops 128 | bytes 1024 | tf_op jit(solution)/shard_map/psum | solution.py:17
  117.1 10.5 %psum.43 = f32[128]{0:T(128)S(1)} all-reduce(f32[128]{0:T(128)S(1)} %psum.42), channel_id=1, replica_groups=mesh['row_0'=4,'row_1'=4,'col'=8] {'row_1'}, use_global_device_ids=true, to_apply=%region_6.7 | all-reduce | flops 128 | bytes 1024 | tf_op jit(solution)/shard_map/psum | solution.py:17
  127.9 30.0 %all_to_all.54 = bf16[8,128,1024]{1,2,0:T(8,128)(2,1)S(1)} all-to-all(bf16[8,128,1024]{1,2,0:T(8,128)(2,1)S(1)} %broadcast_in_dim.89), channel_id=1, replica_groups=mesh['row_0'=4,'row_1'=4,'col'=8] {'col'}, dimensions={0} | all-to-all | bytes 4194304 | tf_op jit(solution)/shard_map/all_to_all | solution.py:22
  161.5 4.4 all-to-all-start.3
  169.2 26.9 %all-to-all-done.3 = bf16[1024,16,64]{0,2,1:T(8,128)(2,1)} async-done(((bf16[1024,16,64]{0,2,1:T(8,128)(2,1)}), bf16[1024,16,64]{0,2,1:T(8,128)(2,1)}, u32[]{:S(2)}, u32[]{:S(2)}) %all-to-all-start.3) | async-done | bytes 2097184 | tf_op jit(solution)/shard_map/all_to_all | solution.py:107
  196.6 52.3 %all_to_all.55 = bf16[16,1024,128]{1,2,0:T(8,128)(2,1)S(1)} all-to-all(bf16[16,1024,128]{1,2,0:T(8,128)(2,1)S(1)} %stack.21), channel_id=1, replica_groups=mesh['row_0'=4,'row_1'=4,'col'=8] {'row_0','row_1'}, dimensions={0} | all-to-all | bytes 8388608 | tf_op jit(solution)/shard_map/all_to_all | solution.py:113
  248.9 7.8 %multiply_add_fusion = f32[1024,2048]{1,0:T(8,128)S(1)} fusion(f32[1024,2048]{1,0:T(8,128)} %param.18, bf16[1024,1024]{0,1:T(8,128)(2,1)} %bitcast.2, bf16[1024,2048]{0,1:T(8,128)(2,1)S(1)} %bitcast.129), kind=kOutput, calls=%fused_computation.5 | convolution fusion | flops 4299161600 | bytes 23068672 | tf_op jit(solution)/shard_map/dot_general | solution.py:115
  265.9 27.2 %all-to-all-done.5 = f32[8,1024,64]{1,2,0:T(8,128)S(1)} async-done(((f32[8,1024,64]{1,2,0:T(8,128)}), f32[8,1024,64]{1,2,0:T(8,128)S(1)}, u32[]{:S(2)}, u32[]{:S(2)}) %all-to-all-start.5) | async-done | bytes 2097184 | tf_op jit(solution)/shard_map/all_to_all | solution.py:22
  298.5 11.4 %all-to-all-done.6 = bf16[16,64,256]{2,1,0:T(8,128)(2,1)} async-done(((bf16[16,64,256]{2,1,0:T(8,128)(2,1)}), bf16[16,64,256]{2,1,0:T(8,128)(2,1)}, u32[]{:S(2)}, u32[]{:S(2)}) %all-to-all-start.6) | async-done | bytes 524320 | tf_op jit(solution)/shard_map/all_to_all | solution.py:22
  311.1 11.7 %cholesky.130 = f32[128,128]{1,0:T(8,128)S(1)} custom-call(f32[128,128]{1,0:T(8,128)S(1)} %cholesky.194), custom_call_target="Cholesky" | custom-call | tf_op jit(solution)/shard_map/jit(cholesky)/cholesky | solution.py:158
  322.8 9.8 %custom-call.13 = f32[1,128,128]{1,2,0:T(8,128)S(1)} custom-call(f32[1,128,128]{2,1,0:T(8,128)S(1)} %get-tuple-element.84), custom_call_target="InvertDiagBlocksLowerTriangular" | custom-call | tf_op jit(solution)/shard_map/jit(cholesky)/cholesky | solution.py:158
  333.1 11.7 %cholesky.147 = f32[128,128]{1,0:T(8,128)S(1)} custom-call(f32[128,128]{1,0:T(8,128)S(1)} %convolution_subtract_fusion.5), custom_call_target="Cholesky" | custom-call | tf_op jit(solution)/shard_map/jit(cholesky)/cholesky | solution.py:158
  347.0 4.3 while.6
  351.3 19.7 %custom-call.14 = f32[2,128,128]{1,2,0:T(8,128)S(1)} custom-call(f32[2,128,128]{2,1,0:T(8,128)S(1)} %get-tuple-element.45), custom_call_target="InvertDiagBlocksLowerTriangular" | custom-call | tf_op jit(solution)/shard_map/jit(_solve_triangular)/triangular_solve | solution.py:159
  376.4 82.4 %all-reduce.8.cloned.1.call-done = (bf16[1,16,64,256]{3,2,1,0:T(8,128)(2,1)}, bf16[1,16,64,256]{3,2,1,0:T(8,128)(2,1)}) async-done(((bf16[1,16,64,256]{3,2,1,0:T(8,128)(2,1)}, bf16[1,16,64,256]{3,2,1,0:T(8,128)(2,1)}), (bf16[1,16,64,256]{3,2,1,0:T(8,128)(2,1)}, bf16[1,16,64,256]{3,2,1,0:T(8,128)(2,1)})) %all-reduce.8.cloned.1.call-update) | async-done | bytes 1048592 | tf_op jit(solution)/shard_map/psum | solution.py:50
  460.2 9.5 %convolution_subtract_fusion.1 = f32[1024,2048]{1,0:T(8,128)S(1)} fusion(f32[1024,2048]{1,0:T(8,128)} %copy-done.4, f32[1024,256]{0,1:T(8,128)S(1)} %get-tuple-element.91, bf16[2048,256]{1,0:T(8,128)(2,1)S(1)} %bitcast.127), kind=kOutput, calls=%fused_computation.8 | convolution fusion | flops 6444548096 | bytes 18874368 | tf_op jit(solution)/shard_map/dot_general | solution.py:54
  475.8 31.7 %all_to_all.56 = f32[8,1024,64]{1,2,0:T(8,128)S(1)} all-to-all(f32[8,1024,64]{1,2,0:T(8,128)S(1)} %broadcast_in_dim.96), channel_id=1, replica_groups=mesh['row_0'=4,'row_1'=4,'col'=8] {'col'}, dimensions={0} | all-to-all | bytes 4194304 | tf_op jit(solution)/shard_map/all_to_all | solution.py:22
  508.5 4.8 all-to-all-start.8
  513.8 10.6 %all-to-all-done.8 = bf16[16,64,256]{2,1,0:T(8,128)(2,1)} async-done(((bf16[16,64,256]{2,1,0:T(8,128)(2,1)}), bf16[16,64,256]{2,1,0:T(8,128)(2,1)}, u32[]{:S(2)}, u32[]{:S(2)}) %all-to-all-start.8) | async-done | bytes 524320 | tf_op jit(solution)/shard_map/all_to_all | solution.py:22
  525.6 11.7 %cholesky.164 = f32[128,128]{1,0:T(8,128)S(1)} custom-call(f32[128,128]{1,0:T(8,128)S(1)} %cholesky.197), custom_call_target="Cholesky" | custom-call | tf_op jit(solution)/shard_map/jit(cholesky)/cholesky | solution.py:158
  537.4 9.8 %custom-call.15 = f32[1,128,128]{1,2,0:T(8,128)S(1)} custom-call(f32[1,128,128]{2,1,0:T(8,128)S(1)} %get-tuple-element.80), custom_call_target="InvertDiagBlocksLowerTriangular" | custom-call | tf_op jit(solution)/shard_map/jit(cholesky)/cholesky | solution.py:158
  547.7 11.7 %cholesky.181 = f32[128,128]{1,0:T(8,128)S(1)} custom-call(f32[128,128]{1,0:T(8,128)S(1)} %convolution_subtract_fusion.4), custom_call_target="Cholesky" | custom-call | tf_op jit(solution)/shard_map/jit(cholesky)/cholesky | solution.py:158
  562.1 4.3 while.7
  566.4 19.7 %custom-call.16 = f32[2,128,128]{1,2,0:T(8,128)S(1)} custom-call(f32[2,128,128]{2,1,0:T(8,128)S(1)} %get-tuple-element.46), custom_call_target="InvertDiagBlocksLowerTriangular" | custom-call | tf_op jit(solution)/shard_map/jit(_solve_triangular)/triangular_solve | solution.py:159
  594.4 79.6 %all-reduce.6.cloned.1.call-done = (bf16[1,16,64,256]{3,2,1,0:T(8,128)(2,1)}, bf16[1,16,64,256]{3,2,1,0:T(8,128)(2,1)}) async-done(((bf16[1,16,64,256]{3,2,1,0:T(8,128)(2,1)}, bf16[1,16,64,256]{3,2,1,0:T(8,128)(2,1)}), (bf16[1,16,64,256]{3,2,1,0:T(8,128)(2,1)}, bf16[1,16,64,256]{3,2,1,0:T(8,128)(2,1)})) %all-reduce.6.cloned.1.call-update) | async-done | bytes 1048592 | tf_op jit(solution)/shard_map/psum | solution.py:50
  675.3 9.5 %convolution_subtract_fusion = f32[1024,2048]{1,0:T(8,128)S(1)} fusion(f32[1024,2048]{1,0:T(8,128)} %scatter.6, f32[1024,256]{0,1:T(8,128)S(1)} %get-tuple-element.94, bf16[2048,256]{1,0:T(8,128)(2,1)S(1)} %bitcast.128), kind=kOutput, calls=%fused_computation.7 | convolution fusion | flops 6444548096 | bytes 18874368 | tf_op jit(solution)/shard_map/dot_general | solution.py:54
  693.3 7.6 %compare_select_fusion = f32[1024,2048]{1,0:T(8,128)} fusion(f32[1024,2048]{1,0:T(8,128)} %scatter.9, s32[2048]{0:T(1024)S(1)} %fusion.41, s32[1024]{0:T(1024)S(1)} %get-tuple-element.95), kind=kLoop, calls=%fused_computation.6 | loop fusion | flops 4194304 | bytes 16789504 | tf_op jit(solution)/shard_map/jit(_where)/select_n | solution.py:194
  (123 shorter events, 78.1 us)
Async XLA Ops:
  6.5 41.7 %copy-start = (bf16[640,1024]{1,0:T(8,128)(2,1)S(1)}, bf16[640,1024]{1,0:T(8,128)(2,1)}, u32[]{:S(2)}) copy-start(bf16[640,1024]{1,0:T(8,128)(2,1)} %param.17) | copy-start | bytes 3932164
  10.1 10.6 %all-to-all-start = ((f32[8,1,64]{2,1,0:T(1,128)}), f32[8,1,64]{2,1,0:T(1,128)S(1)}, u32[]{:S(2)}, u32[]{:S(2)}) async-start(f32[8,1,64]{2,1,0:T(1,128)} %broadcast_in_dim.87), calls=%async_computation | async-start | bytes 8192 | tf_op jit(solution)/shard_map/all_to_all | solution.py:22
  15.5 89.8 %reduce-scatter.2.cloned.1.call-start = ((), (), s32[]{:S(2)}) async-start(), calls=%async_computation.10 | async-start | bytes 9437184 | tf_op jit(solution)/shard_map/reduce_scatter | solution.py:95
  48.2 1.9 copy-start.7
  161.5 34.6 %all-to-all-start.3 = ((bf16[1024,16,64]{0,2,1:T(8,128)(2,1)}), bf16[1024,16,64]{0,2,1:T(8,128)(2,1)}, u32[]{:S(2)}, u32[]{:S(2)}) async-start(bf16[1024,16,64]{0,2,1:T(8,128)(2,1)} %all_to_all.36), calls=%async_computation.4 | async-start | bytes 4194304 | tf_op jit(solution)/shard_map/all_to_all | solution.py:107
  256.7 3.4 copy-start.4
  262.0 31.2 %all-to-all-start.5 = ((f32[8,1024,64]{1,2,0:T(8,128)}), f32[8,1024,64]{1,2,0:T(8,128)S(1)}, u32[]{:S(2)}, u32[]{:S(2)}) async-start(f32[8,1024,64]{1,2,0:T(8,128)} %broadcast_in_dim.91), calls=%async_computation.6 | async-start | bytes 4194304 | tf_op jit(solution)/shard_map/all_to_all | solution.py:22
  294.1 15.8 %all-to-all-start.6 = ((bf16[16,64,256]{2,1,0:T(8,128)(2,1)}), bf16[16,64,256]{2,1,0:T(8,128)(2,1)}, u32[]{:S(2)}, u32[]{:S(2)}) async-start(bf16[16,64,256]{2,1,0:T(8,128)(2,1)} %broadcast_in_dim.92), calls=%async_computation.7 | async-start | bytes 1048576 | tf_op jit(solution)/shard_map/all_to_all | solution.py:22
  298.3 160.5 %all-reduce.8.cloned.1.call-start = ((), (), s32[]{:S(2)}) async-start(), calls=%async_computation.12 | async-start | bytes 2097152 | tf_op jit(solution)/shard_map/psum | solution.py:50
  469.7 3.4 copy-start.2
  474.7 0.8 copy-start.5
  508.5 16.0 %all-to-all-start.8 = ((bf16[16,64,256]{2,1,0:T(8,128)(2,1)}), bf16[16,64,256]{2,1,0:T(8,128)(2,1)}, u32[]{:S(2)}, u32[]{:S(2)}) async-start(bf16[16,64,256]{2,1,0:T(8,128)(2,1)} %broadcast_in_dim.97), calls=%async_computation.9 | async-start | bytes 1048576 | tf_op jit(solution)/shard_map/all_to_all | solution.py:22
  513.3 160.7 %all-reduce.6.cloned.1.call-start = ((), (), s32[]{:S(2)}) async-start(), calls=%async_computation.11 | async-start | bytes 2097152 | tf_op jit(solution)/shard_map/psum | solution.py:50
  587.3 3.6 copy-start.6
  684.8 3.4 copy-start.3
  693.3 7.6 %copy-start.1 = (bf16[640,1024]{1,0:T(8,128)(2,1)S(1)}, bf16[640,1024]{1,0:T(8,128)(2,1)}, u32[]{:S(2)}) copy-start(bf16[640,1024]{1,0:T(8,128)(2,1)} %param.17) | copy-start | bytes 3932164
Sparse Core Ops, SparseCore 0:
  56.4 48.8 reduce-scatter.1
  375.9 82.9 all-reduce.7
  591.0 82.8 all-reduce.5
